TPU v7x, 256 devices: a whole 4x4x8 slice. The times are simulated.
256 devices in a mesh: subj: 4 (over z_hi, core), slab: 64 (over z_lo, y, x).
Axes of the slice: x: 4, y: 4, z: 8 (z_hi: 2, z_lo: 4; z = z_hi * 4 + z_lo), core: 2. Of those that a mesh axis runs over, the one named last changes fastest.
Arguments:
- image: bfloat16 [4, 20, 64, 2, 320], P('subj', None, 'slab'), may hold values from -6 to 6
- upstream: float32 [4, 20, 64, 2, 320], P('subj', None, 'slab'), may hold values from -6 to 6
- coil_maps: float32 [4, 2, 8, 64, 2, 320], P('subj', None, None, 'slab'), may hold values from -1.5 to 1.5
- kernel: float32 [10, 10, 64, 2, 320], P(None, None, None, None, 'slab'), may hold values from -0.5 to 5.5, as said below
- w_first: bfloat16 [3, 3, 3, 64, 20], replicated, may hold values from -0.25 to 0.25
- w_second: bfloat16 [3, 3, 3, 64, 64], replicated, may hold values from -0.15625 to 0.15625
- w_third: bfloat16 [3, 3, 3, 64, 64], replicated, may hold values from -0.15625 to 0.15625
- w_fourth: bfloat16 [3, 3, 3, 64, 64], replicated, may hold values from -0.15625 to 0.15625
- w_last: bfloat16 [3, 3, 3, 20, 64], replicated, may hold values from -0.15625 to 0.15625
Outputs:
- image_grad: float32 [4, 20, 64, 2, 320], P('subj', None, 'slab')
- w_first_grad: float32 [3, 3, 3, 64, 20], replicated
- w_second_grad: float32 [3, 3, 3, 64, 64], replicated
- w_third_grad: float32 [3, 3, 3, 64, 64], replicated
- w_fourth_grad: float32 [3, 3, 3, 64, 64], replicated
- w_last_grad: float32 [3, 3, 3, 20, 64], replicated
Inputs may be any that keep to these rules, and one draw needn't show every extreme that they name: kernel[:, :, kz, x, ky] is a symmetric positive definite 10 x 10 matrix at every k-space point.
All inputs are finite; a program needn't handle non-finite values.
Results may differ from a plain program's by a relative error of at most 0.014.
Values may be sent and summed in bfloat16 or wider, within the bound.
A program may use at most 128 MiB of HBM per device.

v0:
```python
import math
import jax
import jax.numpy as jnp
from jax import lax
from jax.sharding import PartitionSpec as P

ETA_STEP = 0.5
PRECISE = lax.Precision.HIGHEST


def padded_2(block, sides, width):
    for axis, dim in sides:
        count = lax.axis_size(axis)
        forward = [(i, i + 1) for i in range(count - 1)]
        backward = [(target, source) for source, target in forward]
        low = lax.ppermute(
            lax.slice_in_dim(block, block.shape[dim] - width, None, axis=dim), axis, forward
        )
        high = lax.ppermute(lax.slice_in_dim(block, 0, width, axis=dim), axis, backward)
        block = jnp.concatenate([low, block, high], axis=dim)
    return block


def silu_slope(pre_act):
    sigmoid = jax.nn.sigmoid(pre_act)
    return sigmoid * (1.0 + pre_act * (1.0 - sigmoid))


def offsets():
    return [(off_z, off_x, off_y) for off_z in range(3) for off_x in range(3) for off_y in range(3)]


def tap_set(padded_z, forward):
    padded = jnp.pad(padded_z, ((0, 0), (0, 0), (1, 1), (1, 1)))
    count_z = padded_z.shape[1] - 2
    count_x = padded_z.shape[2]
    count_y = padded_z.shape[3]
    pieces = []
    for off_z, off_x, off_y in offsets():
        if forward:
            start_z, start_x, start_y = (off_z, off_x, off_y)
        else:
            start_z, start_x, start_y = (2 - off_z, 2 - off_x, 2 - off_y)
        pieces.append(
            padded[
                :,
                start_z : start_z + count_z,
                start_x : start_x + count_x,
                start_y : start_y + count_y,
            ]
        )
    return jnp.stack(pieces)


def planes_in(activation):
    return padded_2(activation, (("slab", 1),), 1)


def planes_back(delta_grad):
    return padded_2(delta_grad, (("slab", 1),), 1)


def dft_tables(length):
    positions = jnp.arange(length, dtype=jnp.int32)
    products = positions[:, None] * positions[None, :] % length
    angles = products.astype(jnp.float32) * (2.0 * math.pi / length)
    scaling = 1.0 / math.sqrt(length)
    return (jnp.cos(angles) * scaling, jnp.sin(angles) * scaling)


def transform(real_part, imag_part, cosine, sine, pattern, inverse):
    real_cos = jnp.einsum(pattern, real_part, cosine, precision=PRECISE)
    real_sin = jnp.einsum(pattern, real_part, sine, precision=PRECISE)
    imag_cos = jnp.einsum(pattern, imag_part, cosine, precision=PRECISE)
    imag_sin = jnp.einsum(pattern, imag_part, sine, precision=PRECISE)
    if inverse:
        return (real_cos - imag_sin, imag_cos + real_sin)
    return (real_cos + imag_sin, imag_cos - real_sin)


def kspace_mix(arrived, kernel_band, cosine_depth, sine_depth):
    depth_real, depth_imag = transform(
        arrived[0], arrived[1], cosine_depth, sine_depth, "crxyz,zk->crxyk", False
    )
    mixed_real = jnp.einsum("rsxyk,csxyk->crxyk", kernel_band, depth_real, precision=PRECISE)
    mixed_imag = jnp.einsum("rsxyk,csxyk->crxyk", kernel_band, depth_imag, precision=PRECISE)
    back_real, back_imag = transform(
        mixed_real, mixed_imag, cosine_depth, sine_depth, "crxyz,zk->crxyk", True
    )
    return jnp.stack((back_real, back_imag))


def normal_operator(field, maps, kernel_band, tables):
    cosine_rows, sine_rows, cosine_depth, sine_depth = tables
    components = field.shape[0] // 2
    vec_real = field[:components][None]
    vec_imag = field[components:][None]
    map_real = maps[0][:, None]
    map_imag = maps[1][:, None]
    coil_real = map_real * vec_real - map_imag * vec_imag
    coil_imag = map_real * vec_imag + map_imag * vec_real
    spec_real, spec_imag = transform(
        coil_real, coil_imag, cosine_rows, sine_rows, "crzxn,nk->crxkz", False
    )
    spectra = jnp.stack((spec_real, spec_imag))
    arrived = lax.all_to_all(spectra, "slab", split_axis=4, concat_axis=5, tiled=True)
    mixed = kspace_mix(arrived, kernel_band, cosine_depth, sine_depth)
    returned = lax.all_to_all(mixed, "slab", split_axis=5, concat_axis=4, tiled=True)
    back_real, back_imag = transform(
        returned[0], returned[1], cosine_rows, sine_rows, "crxnz,nk->crzxk", True
    )
    out_real = jnp.sum(map_real * back_real + map_imag * back_imag, axis=0)
    out_imag = jnp.sum(map_real * back_imag - map_imag * back_real, axis=0)
    return jnp.concatenate((out_real, out_imag), axis=0)


def body(image, upstream, coil_maps, kernel, w_first, w_second, w_third, w_fourth, w_last):
    weights = (w_first, w_second, w_third, w_fourth, w_last)
    weight_taps = [weight.reshape(27, weight.shape[3], weight.shape[4]) for weight in weights]
    cosine_rows, sine_rows = dft_tables(image.shape[4])
    cosine_depth, sine_depth = dft_tables(kernel.shape[2])
    tables = (cosine_rows, sine_rows, cosine_depth, sine_depth)
    kernel_band = jnp.transpose(kernel, (0, 1, 3, 4, 2))
    local_sums = [jnp.zeros(taps.shape, jnp.float32) for taps in weight_taps]
    direct = upstream[0] - ETA_STEP * normal_operator(
        upstream[0], coil_maps[0], kernel_band, tables
    )
    activation = image[0]
    tap_sets = []
    pre_acts = []
    for level in range(5):
        inputs = tap_set(planes_in(activation), True)
        tap_sets.append(inputs)
        if level < 4:
            pre_act = jnp.einsum(
                "toi,tizxy->ozxy", weight_taps[level], inputs, preferred_element_type=jnp.float32
            )
            pre_acts.append(pre_act)
            activation = jax.nn.silu(pre_act).astype(jnp.bfloat16)
    delta_grad = direct.astype(jnp.bfloat16)
    back_grad = direct
    for level in (4, 3, 2, 1, 0):
        local_sums[level] = jnp.einsum(
            "ozxy,tizxy->toi", delta_grad, tap_sets[level], preferred_element_type=jnp.float32
        )
        shifted = tap_set(planes_back(delta_grad), False)
        back_grad = jnp.einsum(
            "toi,tozxy->izxy", weight_taps[level], shifted, preferred_element_type=jnp.float32
        )
        if level > 0:
            delta_grad = (back_grad * silu_slope(pre_acts[level - 1])).astype(jnp.bfloat16)
    image_grads = [direct + back_grad]
    local_tuple = (local_sums[0], local_sums[1], local_sums[2], local_sums[3], local_sums[4])
    summed = lax.psum(
        (local_tuple[0], local_tuple[1], local_tuple[2], local_tuple[3], local_tuple[4]),
        ("subj", "slab"),
    )
    total_cells = (
        image.shape[0]
        * lax.axis_size("subj")
        * image.shape[2]
        * lax.axis_size("slab")
        * image.shape[3]
        * image.shape[4]
    )
    scaling = 1.0 / math.sqrt(total_cells)
    results = [summed[level].reshape(weights[level].shape) * scaling for level in range(5)]
    return (jnp.stack(image_grads), results[0], results[1], results[2], results[3], results[4])


def solution(mesh):
    in_specs = (
        P("subj", None, "slab", None, None),
        P("subj", None, "slab", None, None),
        P("subj", None, None, "slab", None, None),
        P(None, None, None, None, "slab"),
        P(),
        P(),
        P(),
        P(),
        P(),
    )
    out_specs = (P("subj", None, "slab", None, None), P(), P(), P(), P(), P())
    return jax.shard_map(body, mesh=mesh, in_specs=in_specs, out_specs=out_specs, check_vma=False)
```

profile of v0, /device:TPU:4, one launch (start us, length us, event | category | flops | bytes accessed | tf_op | source)
XLA Modules:
  0.0 623.4 jit_solution(8635704941181876310)
XLA Ops:
  7.2 2.6 collective-permute-start.3
  9.8 3.4 collective-permute-start.2
  14.8 2.8 fusion.160
  21.5 2.7 collective-permute-start.5
  24.2 4.4 collective-permute-start.4
  28.7 2.8 fusion.162
  34.4 3.1 collective-permute-start.7
  37.5 5.0 collective-permute-start.6
  42.5 2.8 fusion.35
  48.3 1.9 collective-permute-start.9
  50.2 6.0 collective-permute-start.8
  56.2 2.8 fusion.36
  63.4 1.9 collective-permute-start.19
  65.4 6.2 %collective-permute-start.18 = (bf16[64,1,2,320]{3,0,2,1:T(8,128)(2,1)S(1)}, bf16[64,1,2,320]{3,0,2,1:T(8,128)(2,1)S(1)}, u32[]{:S(2)}, u32[]{:S(2)}) collective-permute-start(bf16[64,1,2,320]{3,0,2,1:T(8,128)(2,1)S(1)} %fusion.346), channel_id=1, source_target_pairs={{0,1},{1,2},{2,3},{3,4},{4,5},{5,6},{6,7},{7,8},{8,9},{9,10},{10,1... | collective-permute-start | bytes 245768 | tf_op jit(solution)/shard_map/ppermute | solution.py:16
  71.7 5.0 copy.3471
  76.6 8.8 %reshape.355 = f32[64,1,1600]{2,1,0:T(1,128)} reshape(f32[320,2,1,8,2,10]{5,4,3,2,1,0:T(2,128)} %bitcast.1345) | data formatting | bytes 819200
  85.4 23.7 %all-to-all-start = ((f32[64,1,1600]{2,1,0:T(1,128)}), f32[64,1,1600]{2,1,0:T(1,128)S(1)}, u32[]{:S(2)}, u32[]{:S(2)}) async-start(f32[64,1,1600]{2,1,0:T(1,128)} %reshape.355), calls=%async_computation | async-start | bytes 851968 | tf_op jit(solution)/shard_map/all_to_all | solution.py:106
  109.2 4.2 copy.3476
  129.3 1.7 reduce.2
  131.0 9.9 %reshape.356 = f32[320,2,1,8,2,10]{5,4,3,2,1,0:T(2,128)} reshape(f32[64,1600]{1,0:T(8,128)S(1)} %reduce.2) | data formatting | bytes 819200
  140.9 2.8 copy.3472
  143.7 2.7 fusion.349
  146.4 2.3 copy.3474
  148.7 1.6 fusion.96
  150.4 2.3 copy.3473
  153.5 2.7 convolution_subtract_fusion.1
  156.2 3.1 copy.3478
  159.2 12.0 %convolution_bitcast_fusion = f32[8,10,2,5,64]{1,0,4,3,2:T(8,128)} fusion(f32[8,10,2,5,64]{1,0,4,3,2:T(8,128)} %copy.3478, f32[10,10,2,5,64]{1,0,4,3,2:T(8,128)} %copy.3476), kind=kOutput, calls=%fused_computation.26 | convolution fusion | flops 6144000 | bytes 665600 | tf_op jit(solution)/shard_map/rsxyk,csxyk->crxyk/dot_general | solution.py:86
  171.2 2.3 copy.3480
  176.8 3.1 copy.3475
  179.8 11.6 %convolution_bitcast_fusion.1 = f32[8,10,2,5,64]{1,0,4,3,2:T(8,128)} fusion(f32[8,10,2,5,64]{1,0,4,3,2:T(8,128)} %copy.3475, f32[10,10,2,5,64]{1,0,4,3,2:T(8,128)} %copy.3476), kind=kOutput, calls=%fused_computation.27 | convolution fusion | flops 6144000 | bytes 665600 | tf_op jit(solution)/shard_map/rsxyk,csxyk->crxyk/dot_general | solution.py:85
  191.4 2.5 copy.3477
  196.5 5.9 copy.3483
  202.4 6.7 %reshape.357 = f32[64,1,1600]{2,1,0:T(1,128)} reshape(f32[64,2,2,5,8,10]{5,4,3,2,1,0:T(8,128)} %bitcast.1347) | data formatting | bytes 819200
  209.2 10.7 %all-to-all-start.1 = ((f32[64,1,1600]{2,1,0:T(1,128)}), f32[64,1,1600]{2,1,0:T(1,128)S(1)}, u32[]{:S(2)}, u32[]{:S(2)}) async-start(f32[64,1,1600]{2,1,0:T(1,128)} %reshape.357), calls=%async_computation.1 | async-start | bytes 851968 | tf_op jit(solution)/shard_map/all_to_all | solution.py:108
  222.7 8.3 %all-to-all-done.1 = f32[64,1,1600]{2,1,0:T(1,128)S(1)} async-done(((f32[64,1,1600]{2,1,0:T(1,128)}), f32[64,1,1600]{2,1,0:T(1,128)S(1)}, u32[]{:S(2)}, u32[]{:S(2)}) %all-to-all-start.1) | async-done | bytes 409632 | tf_op jit(solution)/shard_map/all_to_all | solution.py:108
  231.1 1.7 reduce.3
  232.7 7.4 %reshape.358 = f32[64,2,2,5,8,10]{5,4,3,2,1,0:T(8,128)} reshape(f32[64,1600]{1,0:T(8,128)S(1)} %reduce.3) | data formatting | bytes 819200
  240.1 2.8 bitcast_bitcast_fusion
  242.9 1.8 fusion.348
  244.8 1.7 copy.3484
  246.5 2.6 copy.3485
  249.1 2.8 fusion.158
  251.9 3.4 copy.3486
  255.4 2.6 copy.3487
  258.0 2.8 fusion.156
  260.8 2.8 fusion.34
  263.7 3.3 add_reduce_fusion
  267.0 3.5 collective-permute-start.1
  270.5 2.5 collective-permute-start
  273.8 2.6 collective-permute-done
  278.3 3.4 collective-permute-start.11
  281.7 2.5 collective-permute-start.10
  284.1 1.8 fusion.28
  285.9 3.6 fusion.37
  292.3 3.4 collective-permute-start.13
  295.7 4.4 collective-permute-start.12
  300.1 1.8 fusion.25
  305.1 1.9 collective-permute-start.15
  307.1 6.2 collective-permute-start.14
  313.3 1.8 fusion.22
  318.1 1.9 collective-permute-start.17
  320.0 6.4 %collective-permute-start.16 = (bf16[64,1,2,320]{3,0,2,1:T(8,128)(2,1)S(1)}, bf16[64,1,2,320]{3,0,2,1:T(8,128)(2,1)S(1)}, u32[]{:S(2)}, u32[]{:S(2)}) collective-permute-start(bf16[64,1,2,320]{3,0,2,1:T(8,128)(2,1)S(1)} %bitcast.1354), channel_id=1, source_target_pairs={{0,1},{1,2},{2,3},{3,4},{4,5},{5,6},{6,7},{7,8},{8,9},{9,10},{10,1... | collective-permute-start | bytes 245768 | tf_op jit(solution)/shard_map/ppermute | solution.py:16
  332.0 275.3 %all-reduce.13.cloned.1.call-done = (f32[27,64,20]{1,0,2:T(8,128)}, f32[27,64,64]{1,2,0:T(8,128)}, f32[27,64,64]{1,2,0:T(8,128)}, f32[27,64,64]{1,2,0:T(8,128)}, f32[27,20,64]{2,1,0:T(8,128)}) async-done(((f32[27,64,20]{1,0,2:T(8,128)}, f32[27,64,64]{1,2,0:T(8,128)}, f32[27,64,64]{1,2,0:T(8,128)}, f32[27,64,64]{1,2,0:T(8,128)}, f32[27,20,64]{2,1,0:T(8,128)}), (f32[27,64,20]{1,0,2:T(8,128)}, ...) | async-done | bytes 1603600 | tf_op jit(solution)/shard_map/psum | solution.py:154
  (395 shorter events, 65.7 us)
Async XLA Ops:
  7.2 54.1 %copy-start = (bf16[3,3,3,64,64]{4,3,2,1,0:T(8,128)(2,1)S(1)}, bf16[3,3,3,64,64]{4,3,2,1,0:T(8,128)(2,1)}, u32[]{:S(2)}) copy-start(bf16[3,3,3,64,64]{4,3,2,1,0:T(8,128)(2,1)} %param.16) | copy-start | bytes 663556
  7.2 12.6 %copy-start.24 = (bf16[1,20,1,2,320]{4,3,2,1,0:T(2,128)(2,1)S(1)}, bf16[1,20,1,2,320]{4,3,2,1,0:T(2,128)(2,1)}, u32[]{:S(2)}) copy-start(bf16[1,20,1,2,320]{4,3,2,1,0:T(2,128)(2,1)} %param.9) | copy-start | bytes 76804
  7.2 13.9 %copy-start.22 = (bf16[3,3,3,64,20]{3,4,2,1,0:T(8,128)(2,1)S(1)}, bf16[3,3,3,64,20]{3,4,2,1,0:T(8,128)(2,1)}, u32[]{:S(2)}) copy-start(bf16[3,3,3,64,20]{3,4,2,1,0:T(8,128)(2,1)} %param.13) | copy-start | bytes 207364
  7.2 10.4 %collective-permute-start.3 = (bf16[20,1,2,320]{3,2,0,1:T(2,128)(2,1)}, bf16[20,1,2,320]{3,2,0,1:T(2,128)(2,1)S(1)}, u32[]{:S(2)}, u32[]{:S(2)}) collective-permute-start(bf16[20,1,2,320]{3,2,0,1:T(2,128)(2,1)} %bitcast.1381), channel_id=1, source_target_pairs={{1,0},{2,1},{3,2},{4,3},{5,4},{6,5},{7,6},{8,7},{9,8},{10,9},{11,1... | collective-permute-start | bytes 76808 | tf_op jit(solution)/shard_map/ppermute | solution.py:19
  9.8 7.8 %collective-permute-start.2 = (bf16[20,1,2,320]{3,2,0,1:T(2,128)(2,1)}, bf16[20,1,2,320]{3,2,0,1:T(2,128)(2,1)S(1)}, u32[]{:S(2)}, u32[]{:S(2)}) collective-permute-start(bf16[20,1,2,320]{3,2,0,1:T(2,128)(2,1)} %bitcast.1382), channel_id=1, source_target_pairs={{0,1},{1,2},{2,3},{3,4},{4,5},{5,6},{6,7},{7,8},{8,9},{9,10},{10,1... | collective-permute-start | bytes 76808 | tf_op jit(solution)/shard_map/ppermute | solution.py:16
  21.1 10.4 %copy-start.10 = (bf16[27,20,1,2,320]{4,3,1,2,0:T(2,128)(2,1)}, bf16[27,20,1,2,320]{4,3,1,2,0:T(2,128)(2,1)S(1)}, u32[]{:S(2)}) copy-start(bf16[27,20,1,2,320]{4,3,1,2,0:T(2,128)(2,1)S(1)} %constant_dynamic-update-slice_fusion.27) | copy-start | bytes 2073604
  21.4 11.2 %copy-start.14 = (f32[64,2,320]{2,0,1:T(8,128)}, f32[64,2,320]{2,0,1:T(8,128)S(1)}, u32[]{:S(2)}) copy-start(f32[64,2,320]{2,0,1:T(8,128)S(1)} %convolution_bitcast_fusion.3) | copy-start | bytes 491524
  21.5 10.0 %collective-permute-start.5 = (bf16[64,1,2,320]{3,0,2,1:T(8,128)(2,1)S(1)}, bf16[64,1,2,320]{3,0,2,1:T(8,128)(2,1)S(1)}, u32[]{:S(2)}, u32[]{:S(2)}) collective-permute-start(bf16[64,1,2,320]{3,0,2,1:T(8,128)(2,1)S(1)} %fusion.343), channel_id=1, source_target_pairs={{1,0},{2,1},{3,2},{4,3},{5,4},{6,5},{7,6},{8,7},{9,8},{10,9},{11,1... | collective-permute-start | bytes 245768 | tf_op jit(solution)/shard_map/ppermute | solution.py:19
  24.2 7.3 %collective-permute-start.4 = (bf16[64,1,2,320]{3,0,2,1:T(8,128)(2,1)S(1)}, bf16[64,1,2,320]{3,0,2,1:T(8,128)(2,1)S(1)}, u32[]{:S(2)}, u32[]{:S(2)}) collective-permute-start(bf16[64,1,2,320]{3,0,2,1:T(8,128)(2,1)S(1)} %fusion.343), channel_id=1, source_target_pairs={{0,1},{1,2},{2,3},{3,4},{4,5},{5,6},{6,7},{7,8},{8,9},{9,10},{10,1... | collective-permute-start | bytes 245768 | tf_op jit(solution)/shard_map/ppermute | solution.py:16
  31.7 2.0 copy-start.19
  33.7 11.6 %copy-start.1 = (bf16[27,64,1,2,320]{4,1,3,2,0:T(8,128)(2,1)}, bf16[27,64,1,2,320]{4,1,3,2,0:T(8,128)(2,1)S(1)}, u32[]{:S(2)}) copy-start(bf16[27,64,1,2,320]{4,1,3,2,0:T(8,128)(2,1)S(1)} %constant_dynamic-update-slice_fusion.54) | copy-start | bytes 6635524
  34.4 11.0 %collective-permute-start.7 = (bf16[64,1,2,320]{3,0,2,1:T(8,128)(2,1)S(1)}, bf16[64,1,2,320]{3,0,2,1:T(8,128)(2,1)S(1)}, u32[]{:S(2)}, u32[]{:S(2)}) collective-permute-start(bf16[64,1,2,320]{3,0,2,1:T(8,128)(2,1)S(1)} %fusion.344), channel_id=1, source_target_pairs={{1,0},{2,1},{3,2},{4,3},{5,4},{6,5},{7,6},{8,7},{9,8},{10,9},{11,1... | collective-permute-start | bytes 245768 | tf_op jit(solution)/shard_map/ppermute | solution.py:19
  37.5 7.8 %collective-permute-start.6 = (bf16[64,1,2,320]{3,0,2,1:T(8,128)(2,1)S(1)}, bf16[64,1,2,320]{3,0,2,1:T(8,128)(2,1)S(1)}, u32[]{:S(2)}, u32[]{:S(2)}) collective-permute-start(bf16[64,1,2,320]{3,0,2,1:T(8,128)(2,1)S(1)} %fusion.344), channel_id=1, source_target_pairs={{0,1},{1,2},{2,3},{3,4},{4,5},{5,6},{6,7},{7,8},{8,9},{9,10},{10,1... | collective-permute-start | bytes 245768 | tf_op jit(solution)/shard_map/ppermute | solution.py:16
  45.6 2.0 copy-start.17
  47.6 11.5 %copy-start.3 = (bf16[27,64,1,2,320]{4,1,3,2,0:T(8,128)(2,1)}, bf16[27,64,1,2,320]{4,1,3,2,0:T(8,128)(2,1)S(1)}, u32[]{:S(2)}) copy-start(bf16[27,64,1,2,320]{4,1,3,2,0:T(8,128)(2,1)S(1)} %constant_dynamic-update-slice_fusion.81) | copy-start | bytes 6635524
  48.3 10.8 %collective-permute-start.9 = (bf16[64,1,2,320]{3,0,2,1:T(8,128)(2,1)S(1)}, bf16[64,1,2,320]{3,0,2,1:T(8,128)(2,1)S(1)}, u32[]{:S(2)}, u32[]{:S(2)}) collective-permute-start(bf16[64,1,2,320]{3,0,2,1:T(8,128)(2,1)S(1)} %fusion.345), channel_id=1, source_target_pairs={{1,0},{2,1},{3,2},{4,3},{5,4},{6,5},{7,6},{8,7},{9,8},{10,9},{11,1... | collective-permute-start | bytes 245768 | tf_op jit(solution)/shard_map/ppermute | solution.py:19
  50.2 8.9 %collective-permute-start.8 = (bf16[64,1,2,320]{3,0,2,1:T(8,128)(2,1)S(1)}, bf16[64,1,2,320]{3,0,2,1:T(8,128)(2,1)S(1)}, u32[]{:S(2)}, u32[]{:S(2)}) collective-permute-start(bf16[64,1,2,320]{3,0,2,1:T(8,128)(2,1)S(1)} %fusion.345), channel_id=1, source_target_pairs={{0,1},{1,2},{2,3},{3,4},{4,5},{5,6},{6,7},{7,8},{8,9},{9,10},{10,1... | collective-permute-start | bytes 245768 | tf_op jit(solution)/shard_map/ppermute | solution.py:16
  61.3 1.5 copy-start.5
  63.4 59.1 %copy-start.8 = (f32[64,2,320]{2,0,1:T(8,128)}, f32[64,2,320]{2,0,1:T(8,128)S(1)}, u32[]{:S(2)}) copy-start(f32[64,2,320]{2,0,1:T(8,128)S(1)} %fusion.49) | copy-start | bytes 491524
  63.4 49.9 %collective-permute-start.19 = (bf16[64,1,2,320]{3,0,2,1:T(8,128)(2,1)S(1)}, bf16[64,1,2,320]{3,0,2,1:T(8,128)(2,1)S(1)}, u32[]{:S(2)}, u32[]{:S(2)}) collective-permute-start(bf16[64,1,2,320]{3,0,2,1:T(8,128)(2,1)S(1)} %fusion.346), channel_id=1, source_target_pairs={{1,0},{2,1},{3,2},{4,3},{5,4},{6,5},{7,6},{8,7},{9,8},{10,9},{11,1... | collective-permute-start | bytes 245768 | tf_op jit(solution)/shard_map/ppermute | solution.py:19
  65.4 48.0 %collective-permute-start.18 = (bf16[64,1,2,320]{3,0,2,1:T(8,128)(2,1)S(1)}, bf16[64,1,2,320]{3,0,2,1:T(8,128)(2,1)S(1)}, u32[]{:S(2)}, u32[]{:S(2)}) collective-permute-start(bf16[64,1,2,320]{3,0,2,1:T(8,128)(2,1)S(1)} %fusion.346), channel_id=1, source_target_pairs={{0,1},{1,2},{2,3},{3,4},{4,5},{5,6},{6,7},{7,8},{8,9},{9,10},{10,1... | collective-permute-start | bytes 245768 | tf_op jit(solution)/shard_map/ppermute | solution.py:16
  76.6 32.5 %copy-start.16 = (f32[10,10,64,2,5]{2,3,4,1,0:T(2,128)S(1)}, f32[10,10,64,2,5]{2,3,4,1,0:T(2,128)}, u32[]{:S(2)}) copy-start(f32[10,10,64,2,5]{2,3,4,1,0:T(2,128)} %param.12) | copy-start | bytes 768004
  85.4 43.4 %all-to-all-start = ((f32[64,1,1600]{2,1,0:T(1,128)}), f32[64,1,1600]{2,1,0:T(1,128)S(1)}, u32[]{:S(2)}, u32[]{:S(2)}) async-start(f32[64,1,1600]{2,1,0:T(1,128)} %reshape.355), calls=%async_computation | async-start | bytes 851968 | tf_op jit(solution)/shard_map/all_to_all | solution.py:106
  191.4 3.3 copy-start.7
  209.2 21.9 %all-to-all-start.1 = ((f32[64,1,1600]{2,1,0:T(1,128)}), f32[64,1,1600]{2,1,0:T(1,128)S(1)}, u32[]{:S(2)}, u32[]{:S(2)}) async-start(f32[64,1,1600]{2,1,0:T(1,128)} %reshape.357), calls=%async_computation.1 | async-start | bytes 851968 | tf_op jit(solution)/shard_map/all_to_all | solution.py:108
  219.9 387.4 %all-reduce.13.cloned.1.call-start = ((), (), s32[]{:S(2)}) async-start(), calls=%async_computation.2 | async-start | bytes 6627328 | tf_op jit(solution)/shard_map/psum | solution.py:154
  258.0 9.0 %copy-start.12 = (f32[1,20,1,2,320]{4,3,2,1,0:T(2,128)S(1)}, f32[1,20,1,2,320]{4,3,2,1,0:T(2,128)}, u32[]{:S(2)}) copy-start(f32[1,20,1,2,320]{4,3,2,1,0:T(2,128)} %param.10) | copy-start | bytes 153604
  267.0 11.0 %copy-start.9 = (f32[64,2,320]{2,0,1:T(8,128)S(1)}, f32[64,2,320]{2,0,1:T(8,128)}, u32[]{:S(2)}) copy-start(f32[64,2,320]{2,0,1:T(8,128)} %copy-done.8) | copy-start | bytes 491524
  267.0 11.0 %copy-start.25 = (bf16[3,3,3,20,64]{4,3,2,1,0:T(8,128)(2,1)S(1)}, bf16[3,3,3,20,64]{4,3,2,1,0:T(8,128)(2,1)}, u32[]{:S(2)}) copy-start(bf16[3,3,3,20,64]{4,3,2,1,0:T(8,128)(2,1)} %param.17) | copy-start | bytes 207364
  267.0 6.8 %collective-permute-start.1 = (bf16[20,1,2,320]{3,0,2,1:T(8,128)(2,1)S(1)}, bf16[20,1,2,320]{3,0,2,1:T(8,128)(2,1)S(1)}, u32[]{:S(2)}, u32[]{:S(2)}) collective-permute-start(bf16[20,1,2,320]{3,0,2,1:T(8,128)(2,1)S(1)} %fusion.234), channel_id=1, source_target_pairs={{1,0},{2,1},{3,2},{4,3},{5,4},{6,5},{7,6},{8,7},{9,8},{10,9},{11,1... | collective-permute-start | bytes 76808 | tf_op jit(solution)/shard_map/ppermute | solution.py:19
  270.5 5.9 collective-permute-start
  276.6 7.5 %copy-start.6 = (bf16[27,64,1,2,320]{4,1,3,2,0:T(8,128)(2,1)S(1)}, bf16[27,64,1,2,320]{4,1,3,2,0:T(8,128)(2,1)}, u32[]{:S(2)}) copy-start(bf16[27,64,1,2,320]{4,1,3,2,0:T(8,128)(2,1)} %copy-done.5) | copy-start | bytes 6635524
  278.3 11.2 %collective-permute-start.11 = (bf16[64,1,2,320]{3,0,2,1:T(8,128)(2,1)S(1)}, bf16[64,1,2,320]{3,0,2,1:T(8,128)(2,1)S(1)}, u32[]{:S(2)}, u32[]{:S(2)}) collective-permute-start(bf16[64,1,2,320]{3,0,2,1:T(8,128)(2,1)S(1)} %bitcast.1356), channel_id=1, source_target_pairs={{1,0},{2,1},{3,2},{4,3},{5,4},{6,5},{7,6},{8,7},{9,8},{10,9},{11,1... | collective-permute-start | bytes 245768 | tf_op jit(solution)/shard_map/ppermute | solution.py:19
  281.7 7.9 %collective-permute-start.10 = (bf16[64,1,2,320]{3,0,2,1:T(8,128)(2,1)S(1)}, bf16[64,1,2,320]{3,0,2,1:T(8,128)(2,1)S(1)}, u32[]{:S(2)}, u32[]{:S(2)}) collective-permute-start(bf16[64,1,2,320]{3,0,2,1:T(8,128)(2,1)S(1)} %bitcast.1357), channel_id=1, source_target_pairs={{0,1},{1,2},{2,3},{3,4},{4,5},{5,6},{6,7},{7,8},{8,9},{9,10},{10,1... | collective-permute-start | bytes 245768 | tf_op jit(solution)/shard_map/ppermute | solution.py:16
  291.2 8.9 %copy-start.4 = (bf16[27,64,1,2,320]{4,1,3,2,0:T(8,128)(2,1)S(1)}, bf16[27,64,1,2,320]{4,1,3,2,0:T(8,128)(2,1)}, u32[]{:S(2)}) copy-start(bf16[27,64,1,2,320]{4,1,3,2,0:T(8,128)(2,1)} %copy-done.3) | copy-start | bytes 6635524
  292.3 9.6 %collective-permute-start.13 = (bf16[64,1,2,320]{3,0,2,1:T(8,128)(2,1)S(1)}, bf16[64,1,2,320]{3,0,2,1:T(8,128)(2,1)S(1)}, u32[]{:S(2)}, u32[]{:S(2)}) collective-permute-start(bf16[64,1,2,320]{3,0,2,1:T(8,128)(2,1)S(1)} %bitcast.1359), channel_id=1, source_target_pairs={{1,0},{2,1},{3,2},{4,3},{5,4},{6,5},{7,6},{8,7},{9,8},{10,9},{11,1... | collective-permute-start | bytes 245768 | tf_op jit(solution)/shard_map/ppermute | solution.py:19
  295.7 6.6 %collective-permute-start.12 = (bf16[64,1,2,320]{3,0,2,1:T(8,128)(2,1)S(1)}, bf16[64,1,2,320]{3,0,2,1:T(8,128)(2,1)S(1)}, u32[]{:S(2)}, u32[]{:S(2)}) collective-permute-start(bf16[64,1,2,320]{3,0,2,1:T(8,128)(2,1)S(1)} %bitcast.1360), channel_id=1, source_target_pairs={{0,1},{1,2},{2,3},{3,4},{4,5},{5,6},{6,7},{7,8},{8,9},{9,10},{10,1... | collective-permute-start | bytes 245768 | tf_op jit(solution)/shard_map/ppermute | solution.py:16
  302.5 2.0 copy-start.18
  304.0 9.2 %copy-start.2 = (bf16[27,64,1,2,320]{4,1,3,2,0:T(8,128)(2,1)S(1)}, bf16[27,64,1,2,320]{4,1,3,2,0:T(8,128)(2,1)}, u32[]{:S(2)}) copy-start(bf16[27,64,1,2,320]{4,1,3,2,0:T(8,128)(2,1)} %copy-done.1) | copy-start | bytes 6635524
  305.1 9.9 %collective-permute-start.15 = (bf16[64,1,2,320]{3,0,2,1:T(8,128)(2,1)S(1)}, bf16[64,1,2,320]{3,0,2,1:T(8,128)(2,1)S(1)}, u32[]{:S(2)}, u32[]{:S(2)}) collective-permute-start(bf16[64,1,2,320]{3,0,2,1:T(8,128)(2,1)S(1)} %bitcast.1362), channel_id=1, source_target_pairs={{1,0},{2,1},{3,2},{4,3},{5,4},{6,5},{7,6},{8,7},{9,8},{10,9},{11,1... | collective-permute-start | bytes 245768 | tf_op jit(solution)/shard_map/ppermute | solution.py:19
  307.1 8.2 %collective-permute-start.14 = (bf16[64,1,2,320]{3,0,2,1:T(8,128)(2,1)S(1)}, bf16[64,1,2,320]{3,0,2,1:T(8,128)(2,1)S(1)}, u32[]{:S(2)}, u32[]{:S(2)}) collective-permute-start(bf16[64,1,2,320]{3,0,2,1:T(8,128)(2,1)S(1)} %bitcast.1363), channel_id=1, source_target_pairs={{0,1},{1,2},{2,3},{3,4},{4,5},{5,6},{6,7},{7,8},{8,9},{9,10},{10,1... | collective-permute-start | bytes 245768 | tf_op jit(solution)/shard_map/ppermute | solution.py:16
  315.5 2.0 copy-start.15
  315.5 2.0 copy-start.20
  317.0 9.5 %copy-start.11 = (bf16[27,20,1,2,320]{4,3,1,2,0:T(2,128)(2,1)S(1)}, bf16[27,20,1,2,320]{4,3,1,2,0:T(2,128)(2,1)}, u32[]{:S(2)}) copy-start(bf16[27,20,1,2,320]{4,3,1,2,0:T(2,128)(2,1)} %copy-done.10) | copy-start | bytes 2073604
  318.1 9.5 %collective-permute-start.17 = (bf16[64,1,2,320]{3,0,2,1:T(8,128)(2,1)S(1)}, bf16[64,1,2,320]{3,0,2,1:T(8,128)(2,1)S(1)}, u32[]{:S(2)}, u32[]{:S(2)}) collective-permute-start(bf16[64,1,2,320]{3,0,2,1:T(8,128)(2,1)S(1)} %bitcast.1353), channel_id=1, source_target_pairs={{1,0},{2,1},{3,2},{4,3},{5,4},{6,5},{7,6},{8,7},{9,8},{10,9},{11,1... | collective-permute-start | bytes 245768 | tf_op jit(solution)/shard_map/ppermute | solution.py:19
  320.0 8.6 %collective-permute-start.16 = (bf16[64,1,2,320]{3,0,2,1:T(8,128)(2,1)S(1)}, bf16[64,1,2,320]{3,0,2,1:T(8,128)(2,1)S(1)}, u32[]{:S(2)}, u32[]{:S(2)}) collective-permute-start(bf16[64,1,2,320]{3,0,2,1:T(8,128)(2,1)S(1)} %bitcast.1354), channel_id=1, source_target_pairs={{0,1},{1,2},{2,3},{3,4},{4,5},{5,6},{6,7},{7,8},{8,9},{9,10},{10,1... | collective-permute-start | bytes 245768 | tf_op jit(solution)/shard_map/ppermute | solution.py:16
  328.9 2.0 copy-start.23
  607.3 4.4 copy-start.13
  613.2 2.4 copy-start.21
Sparse Core Ops, SparseCore 0:
  327.8 279.5 all-reduce.12
where the time goes:
time: 632 us; the launch traced here: 623 us
  waiting for transfers between devices  288 us (46%)
  local copies, waits for them, and re-layouts  127 us (20%)
  starting transfers between devices  108 us (17%)
  matrix products  72.3 us (11%)
  between operations  16.6 us (3%)
  other arithmetic  11.8 us (2%)
    psum x1, waiting for transfers between devices, body(): lax.psum((local_tuple[0], local_tuple[1], local_tuple[2], local_tuple[3],...  275 us
    unnamed x315, local copies, waits for them, and re-layouts  71.1 us
    ppermute x10, starting transfers between devices, padded_2(): lax.ppermute(lax.slice_in_dim(block, block.shape[dim] - width, None, axis...  47.1 us
    ppermute x10, starting transfers between devices, padded_2(): lax.ppermute(lax.slice_in_dim(block, 0, width, axis=dim), axis, backward)  26.3 us
    all_to_all x1, starting transfers between devices, normal_operator(): lax.all_to_all(spectra, 'slab', split_axis=4, concat_axis=5, tiled=True)  23.7 us
  transfers between devices with their start and end apart: 23, of which 6 were waited for; matrix products, arithmetic and copies ran while one was open for 10% of the time, Pallas kernels for 0%

commit v1 on v0

--- a/solution.py
+++ b/solution.py
@@ -152,8 +152,10 @@
     image_grads = [direct + back_grad]
     local_tuple = (local_sums[0], local_sums[1], local_sums[2], local_sums[3], local_sums[4])
     summed = lax.psum(
-        (local_tuple[0], local_tuple[1], local_tuple[2], local_tuple[3], local_tuple[4]),
-        ("subj", "slab"),
+        lax.psum(
+            (local_tuple[0], local_tuple[1], local_tuple[2], local_tuple[3], local_tuple[4]), "subj"
+        ),
+        "slab",
     )
     total_cells = (
         image.shape[0]

time: 632 us -> 1220 us (1.93)
  waiting for transfers between devices: 288 us -> 857 us
  local copies, waits for them, and re-layouts: 127 us -> 144 us
    psum x0 -> x1, waiting for transfers between devices: none -> 719 us  [body(): lax.psum(lax.psum((local_tuple[0], local_tuple[1], local_tuple[2], local_...]
    psum x1, waiting for transfers between devices: 275 us -> 125 us  [body(): lax.psum((local_tuple[0], local_tuple[1], local_tuple[2], local_tuple[3],...]
    unnamed x315, local copies, waits for them, and re-layouts: 71.1 us -> 87.5 us
  transfers between devices with their start and end apart: 23 -> 24, of which waited for: 6 -> 7; matrix products, arithmetic and copies ran while one was open for 10% -> 7% of each run, Pallas kernels for 0% -> 0%
where the time goes in v1:
time: 1220 us; the launch traced here: 1210 us
  waiting for transfers between devices  857 us (70%)
  local copies, waits for them, and re-layouts  144 us (12%)
  starting transfers between devices  108 us (9%)
  matrix products  74 us (6%)
  between operations  16.4 us (1%)
    psum x1, waiting for transfers between devices, body(): lax.psum(lax.psum((local_tuple[0], local_tuple[1], local_tuple[2], local_...  719 us
    psum x1, waiting for transfers between devices, body(): lax.psum((local_tuple[0], local_tuple[1], local_tuple[2], local_tuple[3],...  125 us
    unnamed x315, local copies, waits for them, and re-layouts  87.5 us
    ppermute x10, starting transfers between devices, padded_2(): lax.ppermute(lax.slice_in_dim(block, block.shape[dim] - width, None, axis...  47.1 us
    ppermute x10, starting transfers between devices, padded_2(): lax.ppermute(lax.slice_in_dim(block, 0, width, axis=dim), axis, backward)  26.3 us
  transfers between devices with their start and end apart: 24, of which 7 were waited for; matrix products, arithmetic and copies ran while one was open for 7% of the time, Pallas kernels for 0%

profile of v1, /device:TPU:4, one launch (start us, length us, event | category | flops | bytes accessed | tf_op | source)
XLA Modules:
  0.0 1210.9 jit_solution(384143983951208783)
XLA Ops:
  7.2 2.6 collective-permute-start.3
  9.8 3.4 collective-permute-start.2
  14.8 2.8 fusion.160
  21.5 2.7 collective-permute-start.5
  24.2 4.4 collective-permute-start.4
  28.7 2.8 fusion.162
  34.4 3.1 collective-permute-start.7
  37.5 5.0 collective-permute-start.6
  42.5 2.8 fusion.35
  48.3 1.9 collective-permute-start.9
  50.2 6.0 collective-permute-start.8
  56.2 2.8 fusion.36
  63.4 1.9 collective-permute-start.19
  65.4 6.2 collective-permute-start.18
  71.7 5.0 copy.3471
  76.7 8.8 reshape.355
  85.5 23.7 %all-to-all-start = ((f32[64,1,1600]{2,1,0:T(1,128)}), f32[64,1,1600]{2,1,0:T(1,128)S(1)}, u32[]{:S(2)}, u32[]{:S(2)}) async-start(f32[64,1,1600]{2,1,0:T(1,128)} %reshape.355), calls=%async_computation | async-start | bytes 851968 | tf_op jit(solution)/shard_map/all_to_all | solution.py:106
  109.2 4.1 copy.3476
  131.0 9.9 reshape.356
  140.9 2.8 copy.3472
  143.7 2.8 fusion.349
  146.5 2.3 copy.3474
  150.4 2.3 copy.3473
  153.5 2.7 convolution_subtract_fusion.1
  156.2 3.1 copy.3478
  159.3 12.0 convolution_bitcast_fusion
  171.3 2.3 copy.3480
  176.8 3.1 copy.3475
  179.9 11.6 convolution_bitcast_fusion.1
  191.5 2.5 copy.3477
  196.6 5.9 copy.3483
  202.5 6.7 reshape.357
  209.2 10.7 all-to-all-start.1
  222.8 8.3 all-to-all-done.1
  231.1 1.7 reduce.3
  232.8 7.4 reshape.358
  240.2 2.8 bitcast_bitcast_fusion
  243.0 1.8 fusion.348
  244.8 1.7 copy.3484
  246.5 2.6 copy.3485
  249.2 2.8 fusion.158
  252.0 3.4 copy.3486
  255.4 2.6 copy.3487
  258.1 2.8 fusion.156
  260.9 2.8 fusion.34
  263.7 3.3 add_reduce_fusion
  267.1 3.5 collective-permute-start.1
  270.6 2.5 collective-permute-start
  273.9 2.6 collective-permute-done
  278.3 3.4 collective-permute-start.11
  281.7 2.5 collective-permute-start.10
  284.2 1.8 fusion.28
  286.0 3.6 fusion.37
  292.4 3.4 collective-permute-start.13
  295.7 4.4 collective-permute-start.12
  300.2 1.8 fusion.25
  305.2 1.9 collective-permute-start.15
  307.1 6.2 collective-permute-start.14
  313.3 1.8 fusion.22
  318.2 1.9 collective-permute-start.17
  320.1 6.4 collective-permute-start.16
  343.6 124.7 %all-reduce.17.cloned.1.call-done = (f32[27,64,20]{1,0,2:T(8,128)}, f32[27,64,64]{1,2,0:T(8,128)}, f32[27,64,64]{1,2,0:T(8,128)}, f32[27,64,64]{1,2,0:T(8,128)}, f32[27,20,64]{2,1,0:T(8,128)}) async-done(((f32[27,64,20]{1,0,2:T(8,128)}, f32[27,64,64]{1,2,0:T(8,128)}, f32[27,64,64]{1,2,0:T(8,128)}, f32[27,64,64]{1,2,0:T(8,128)}, f32[27,20,64]{2,1,0:T(8,128)}), (f32[27,64,20]{1,0,2:T(8,128)}, ...) | async-done | bytes 1603600 | tf_op jit(solution)/shard_map/psum | solution.py:155
  472.5 2.3 fusion.87
  475.4 719.5 %all-reduce.15.cloned.1.call-done = (f32[27,64,20]{1,0,2:T(8,128)}, f32[27,64,64]{1,2,0:T(8,128)}, f32[27,64,64]{1,2,0:T(8,128)}, f32[27,64,64]{1,2,0:T(8,128)}, f32[27,20,64]{2,1,0:T(8,128)}) async-done(((f32[27,64,20]{1,0,2:T(8,128)}, f32[27,64,64]{1,2,0:T(8,128)}, f32[27,64,64]{1,2,0:T(8,128)}, f32[27,64,64]{1,2,0:T(8,128)}, f32[27,20,64]{2,1,0:T(8,128)}), (f32[27,64,20]{1,0,2:T(8,128)}, ...) | async-done | bytes 1603600 | tf_op jit(solution)/shard_map/psum | solution.py:154
  (398 shorter events, 85.5 us)
Async XLA Ops:
  7.2 54.1 %copy-start = (bf16[3,3,3,64,64]{4,3,2,1,0:T(8,128)(2,1)S(1)}, bf16[3,3,3,64,64]{4,3,2,1,0:T(8,128)(2,1)}, u32[]{:S(2)}) copy-start(bf16[3,3,3,64,64]{4,3,2,1,0:T(8,128)(2,1)} %param.16) | copy-start | bytes 663556
  7.2 12.6 %copy-start.24 = (bf16[1,20,1,2,320]{4,3,2,1,0:T(2,128)(2,1)S(1)}, bf16[1,20,1,2,320]{4,3,2,1,0:T(2,128)(2,1)}, u32[]{:S(2)}) copy-start(bf16[1,20,1,2,320]{4,3,2,1,0:T(2,128)(2,1)} %param.9) | copy-start | bytes 76804
  7.2 13.9 %copy-start.22 = (bf16[3,3,3,64,20]{3,4,2,1,0:T(8,128)(2,1)S(1)}, bf16[3,3,3,64,20]{3,4,2,1,0:T(8,128)(2,1)}, u32[]{:S(2)}) copy-start(bf16[3,3,3,64,20]{3,4,2,1,0:T(8,128)(2,1)} %param.13) | copy-start | bytes 207364
  7.2 10.4 collective-permute-start.3
  9.8 7.8 collective-permute-start.2
  21.1 10.4 copy-start.10
  21.4 11.2 copy-start.14
  21.5 10.0 collective-permute-start.5
  24.2 7.3 collective-permute-start.4
  31.7 2.0 copy-start.19
  33.7 11.6 copy-start.1
  34.4 11.0 collective-permute-start.7
  37.5 7.8 collective-permute-start.6
  45.6 2.0 copy-start.17
  47.6 11.5 copy-start.3
  48.3 10.8 collective-permute-start.9
  50.2 8.9 collective-permute-start.8
  61.3 1.5 copy-start.5
  63.4 59.2 %copy-start.8 = (f32[64,2,320]{2,0,1:T(8,128)}, f32[64,2,320]{2,0,1:T(8,128)S(1)}, u32[]{:S(2)}) copy-start(f32[64,2,320]{2,0,1:T(8,128)S(1)} %fusion.49) | copy-start | bytes 491524
  63.4 49.9 %collective-permute-start.19 = (bf16[64,1,2,320]{3,0,2,1:T(8,128)(2,1)S(1)}, bf16[64,1,2,320]{3,0,2,1:T(8,128)(2,1)S(1)}, u32[]{:S(2)}, u32[]{:S(2)}) collective-permute-start(bf16[64,1,2,320]{3,0,2,1:T(8,128)(2,1)S(1)} %fusion.346), channel_id=1, source_target_pairs={{1,0},{2,1},{3,2},{4,3},{5,4},{6,5},{7,6},{8,7},{9,8},{10,9},{11,1... | collective-permute-start | bytes 245768 | tf_op jit(solution)/shard_map/ppermute | solution.py:19
  65.4 48.0 %collective-permute-start.18 = (bf16[64,1,2,320]{3,0,2,1:T(8,128)(2,1)S(1)}, bf16[64,1,2,320]{3,0,2,1:T(8,128)(2,1)S(1)}, u32[]{:S(2)}, u32[]{:S(2)}) collective-permute-start(bf16[64,1,2,320]{3,0,2,1:T(8,128)(2,1)S(1)} %fusion.346), channel_id=1, source_target_pairs={{0,1},{1,2},{2,3},{3,4},{4,5},{5,6},{6,7},{7,8},{8,9},{9,10},{10,1... | collective-permute-start | bytes 245768 | tf_op jit(solution)/shard_map/ppermute | solution.py:16
  76.7 32.5 %copy-start.16 = (f32[10,10,64,2,5]{2,3,4,1,0:T(2,128)S(1)}, f32[10,10,64,2,5]{2,3,4,1,0:T(2,128)}, u32[]{:S(2)}) copy-start(f32[10,10,64,2,5]{2,3,4,1,0:T(2,128)} %param.12) | copy-start | bytes 768004
  85.5 43.4 %all-to-all-start = ((f32[64,1,1600]{2,1,0:T(1,128)}), f32[64,1,1600]{2,1,0:T(1,128)S(1)}, u32[]{:S(2)}, u32[]{:S(2)}) async-start(f32[64,1,1600]{2,1,0:T(1,128)} %reshape.355), calls=%async_computation | async-start | bytes 851968 | tf_op jit(solution)/shard_map/all_to_all | solution.py:106
  191.5 3.3 copy-start.7
  209.2 21.9 %all-to-all-start.1 = ((f32[64,1,1600]{2,1,0:T(1,128)}), f32[64,1,1600]{2,1,0:T(1,128)S(1)}, u32[]{:S(2)}, u32[]{:S(2)}) async-start(f32[64,1,1600]{2,1,0:T(1,128)} %reshape.357), calls=%async_computation.1 | async-start | bytes 851968 | tf_op jit(solution)/shard_map/all_to_all | solution.py:108
  220.0 248.3 %all-reduce.17.cloned.1.call-start = ((), (), s32[]{:S(2)}) async-start(), calls=%async_computation.3 | async-start | bytes 6627328 | tf_op jit(solution)/shard_map/psum | solution.py:155
  258.1 9.0 copy-start.12
  267.0 11.0 copy-start.9
  267.0 11.0 copy-start.25
  267.1 6.8 collective-permute-start.1
  270.6 5.9 collective-permute-start
  276.7 7.5 copy-start.6
  278.3 11.2 collective-permute-start.11
  281.7 7.9 collective-permute-start.10
  291.3 8.9 copy-start.4
  292.4 9.6 collective-permute-start.13
  295.7 6.6 collective-permute-start.12
  302.6 2.0 copy-start.18
  304.1 9.2 copy-start.2
  305.2 9.9 collective-permute-start.15
  307.1 8.2 collective-permute-start.14
  315.5 2.0 copy-start.15
  315.5 2.0 copy-start.20
  317.1 9.5 copy-start.11
  318.2 9.6 collective-permute-start.17
  320.1 8.6 collective-permute-start.16
  327.7 867.2 %all-reduce.15.cloned.1.call-start = ((), (), s32[]{:S(2)}) async-start(), calls=%async_computation.2 | async-start | bytes 6627328 | tf_op jit(solution)/shard_map/psum | solution.py:154
  340.8 131.7 %copy-start.23 = (bf16[3,3,3,64,20]{3,4,2,1,0:T(8,128)(2,1)S(1)}, bf16[3,3,3,64,20]{3,4,2,1,0:T(8,128)(2,1)}, u32[]{:S(2)}) copy-start(bf16[3,3,3,64,20]{3,4,2,1,0:T(8,128)(2,1)} %param.13) | copy-start | bytes 207364
  1194.9 4.4 copy-start.13
  1200.7 2.4 copy-start.21
Sparse Core Ops, SparseCore 0:
  327.8 140.4 all-reduce.16
  471.6 723.2 all-reduce.14
